TPU v7x, 256 devices: a whole 4x4x8 slice. The times are simulated.
256 devices in a mesh: blk: 16 (over y, z_lo, core), head: 16 (over x, z_hi).
Axes of the slice: x: 4, y: 4, z: 8 (z_hi: 4, z_lo: 2; z = z_hi * 2 + z_lo), core: 2. Of those that a mesh axis runs over, the one named last changes fastest.
Arguments:
- query: bfloat16 [16384, 2, 1024], P(('blk', 'head')), may hold values from -6.59375 to 6.59375
- key_in: bfloat16 [16384, 2, 1024], P(('blk', 'head')), may hold values from -6.59375 to 6.59375
- value: bfloat16 [16384, 2, 1024], P(('blk', 'head')), may hold values from -6 to 6
- output: bfloat16 [16384, 2, 1024], P(('blk', 'head')), may hold values from -2 to 2
- grad_out: bfloat16 [16384, 2, 1024], P(('blk', 'head')), may hold values from -192 to 192
- log_sum_exp: float32 [16, 2, 16384], P(None, None, ('blk', 'head')), as said below
Outputs:
- grad_query: bfloat16 [16384, 2, 1024], P(('blk', 'head'))
- grad_key: bfloat16 [16384, 2, 1024], P(('blk', 'head'))
- grad_value: bfloat16 [16384, 2, 1024], P(('blk', 'head'))
Inputs may be any that keep to these rules, and one draw needn't show every extreme that they name: `log_sum_exp`: each entry lies between log(16384) + 0.5 and log(16384) + 1.5.
All inputs are finite; a program needn't handle non-finite values.
Results may differ from a plain program's by a relative error of at most 0.0054.
Values may be sent and summed in bfloat16 or wider, within the bound.
A program may use at most 192 MiB of HBM per device.

v0:
```python
import jax
import jax.numpy as jnp
from jax import lax
from jax.sharding import PartitionSpec as P


def shifted(block, axis, distance):
    devices = range(lax.axis_size(axis))
    route = [((i - distance) % len(devices), i) for i in devices]
    return lax.ppermute(block, axis, route)


def block_terms(queries, grad_rows, lse_rows, dot_rows, keys_blk, values_blk, score_scale):
    scores = (
        jnp.einsum("qshd,kshd->hsqk", queries, keys_blk, preferred_element_type=jnp.float32)
        * score_scale
    )
    attn_probs = jnp.exp(scores - lse_rows[:, :, :, None])
    grad_probs = jnp.einsum(
        "qshd,kshd->hsqk", grad_rows, values_blk, preferred_element_type=jnp.float32
    )
    grad_scores = (attn_probs * (grad_probs - dot_rows[:, :, :, None]) * score_scale).astype(
        jnp.bfloat16
    )
    return (attn_probs, grad_scores)


def shards(query, key_in, value, output, grad_out, log_sum_exp):
    frame_rows, seq_count, width_all = query.shape
    head_total = log_sum_exp.shape[0]
    head_size = width_all // head_total
    head_local = head_total // lax.axis_size("head")
    score_scale = head_size ** (-0.5)
    queries, keys_blk, values_blk, grad_rows, out_rows = (
        lax.all_to_all(query, "head", split_axis=2, concat_axis=0, tiled=True),
        lax.all_to_all(key_in, "head", split_axis=2, concat_axis=0, tiled=True),
        lax.all_to_all(value, "head", split_axis=2, concat_axis=0, tiled=True),
        lax.all_to_all(grad_out, "head", split_axis=2, concat_axis=0, tiled=True),
        lax.all_to_all(output, "head", split_axis=2, concat_axis=0, tiled=True),
    )
    lse_rows = lax.all_to_all(log_sum_exp, "head", split_axis=0, concat_axis=2, tiled=True)
    block_rows = queries.shape[0]
    products = out_rows.astype(jnp.float32) * grad_rows.astype(jnp.float32)
    dot_rows = jnp.sum(
        products.reshape(block_rows, seq_count, head_local, head_size), axis=3
    ).transpose(2, 1, 0)
    shape_four = (block_rows, seq_count, head_local, head_size)
    queries = queries.reshape(shape_four)
    keys_blk = keys_blk.reshape(shape_four)
    values_blk = values_blk.reshape(shape_four)
    grad_rows = grad_rows.reshape(shape_four)
    zeros_init = jnp.zeros(shape_four, jnp.float32)

    def cycle_turn(turn_index, carry):
        keys_now, values_now, grad_keys, grad_values, grad_queries = carry
        attn_probs, grad_scores = block_terms(
            queries, grad_rows, lse_rows, dot_rows, keys_now, values_now, score_scale
        )
        grad_queries = grad_queries + jnp.einsum(
            "hsqk,kshd->qshd", grad_scores, keys_now, preferred_element_type=jnp.float32
        )
        grad_keys = grad_keys + jnp.einsum(
            "hsqk,qshd->kshd", grad_scores, queries, preferred_element_type=jnp.float32
        )
        grad_values = grad_values + jnp.einsum(
            "hsqk,qshd->kshd",
            attn_probs.astype(jnp.bfloat16),
            grad_rows,
            preferred_element_type=jnp.float32,
        )
        keys_now, values_now = shifted((keys_now, values_now), "blk", 1)
        grad_keys, grad_values = shifted((grad_keys, grad_values), "blk", 1)
        return (keys_now, values_now, grad_keys, grad_values, grad_queries)

    start_carry = (keys_blk, values_blk, zeros_init, zeros_init, zeros_init)
    final_carry = lax.fori_loop(0, lax.axis_size("blk"), cycle_turn, start_carry)
    grad_keys, grad_values, grad_queries = (final_carry[2], final_carry[3], final_carry[4])
    flat_shape = (block_rows, seq_count, head_local * head_size)
    grad_q_low = grad_queries.reshape(flat_shape).astype(jnp.bfloat16)
    grad_k_low = grad_keys.reshape(flat_shape).astype(jnp.bfloat16)
    grad_v_low = grad_values.reshape(flat_shape).astype(jnp.bfloat16)
    grad_query, grad_key, grad_value = (
        lax.all_to_all(grad_q_low, "head", split_axis=0, concat_axis=2, tiled=True),
        lax.all_to_all(grad_k_low, "head", split_axis=0, concat_axis=2, tiled=True),
        lax.all_to_all(grad_v_low, "head", split_axis=0, concat_axis=2, tiled=True),
    )
    return (grad_query, grad_key, grad_value)


def solution(mesh):
    placed = (
        P(("blk", "head"), None, None),
        P(("blk", "head"), None, None),
        P(("blk", "head"), None, None),
        P(("blk", "head"), None, None),
        P(("blk", "head"), None, None),
        P(None, None, ("blk", "head")),
    )
    return jax.shard_map(
        shards,
        mesh=mesh,
        in_specs=placed,
        out_specs=(
            P(("blk", "head"), None, None),
            P(("blk", "head"), None, None),
            P(("blk", "head"), None, None),
        ),
        check_vma=False,
    )
```

profile of v0, /device:TPU:0, one launch (start us, length us, event | category | flops | bytes accessed | tf_op | source)
XLA Modules:
  0.0 676.1 jit_solution(14713670143637701352)
XLA Ops:
  2.1 9.3 %all-to-all-start.3 = ((f32[16,1,128]{2,1,0:T(1,128)}), f32[16,1,128]{2,1,0:T(1,128)S(1)}, u32[]{:S(2)}, u32[]{:S(2)}) async-start(f32[16,1,128]{2,1,0:T(1,128)} %reshape.89), calls=%async_computation.3 | async-start | bytes 16384 | tf_op jit(solution)/shard_map/all_to_all | solution.py:41
  13.9 7.3 %all-to-all-done.3 = f32[16,1,128]{2,1,0:T(1,128)S(1)} async-done(((f32[16,1,128]{2,1,0:T(1,128)}), f32[16,1,128]{2,1,0:T(1,128)S(1)}, u32[]{:S(2)}, u32[]{:S(2)}) %all-to-all-start.3) | async-done | bytes 8224 | tf_op jit(solution)/shard_map/all_to_all | solution.py:41
  27.4 9.7 %all-to-all-done.4 = bf16[16,2,4096]{2,1,0:T(2,128)(2,1)S(1)} async-done(((bf16[16,2,4096]{2,1,0:T(2,128)(2,1)}), bf16[16,2,4096]{2,1,0:T(2,128)(2,1)S(1)}, u32[]{:S(2)}, u32[]{:S(2)}) %all-to-all-start.4) | async-done | bytes 262176 | tf_op jit(solution)/shard_map/all_to_all | solution.py:38
  43.2 9.1 %all-to-all-done.5 = bf16[16,2,4096]{2,1,0:T(2,128)(2,1)S(1)} async-done(((bf16[16,2,4096]{2,1,0:T(2,128)(2,1)}), bf16[16,2,4096]{2,1,0:T(2,128)(2,1)S(1)}, u32[]{:S(2)}, u32[]{:S(2)}) %all-to-all-start.5) | async-done | bytes 262176 | tf_op jit(solution)/shard_map/all_to_all | solution.py:39
  58.4 9.5 %all-to-all-done = bf16[16,2,4096]{2,1,0:T(2,128)(2,1)S(1)} async-done(((bf16[16,2,4096]{2,1,0:T(2,128)(2,1)}), bf16[16,2,4096]{2,1,0:T(2,128)(2,1)S(1)}, u32[]{:S(2)}, u32[]{:S(2)}) %all-to-all-start) | async-done | bytes 262176 | tf_op jit(solution)/shard_map/all_to_all | solution.py:36
  74.8 11.2 %copy.42 = bf16[64,2,16,64]{1,0,3,2:T(8,128)(2,1)} copy(bf16[64,2,16,64]{0,1,3,2:T(2,128)(2,1)S(1)} %bitcast.146) | data formatting | bytes 524288 | tf_op jit(solution)/shard_map/all_to_all | solution.py:38
  86.4 14.0 %copy.45 = f32[64,2,16,64]{1,0,3,2:T(8,128)} copy(bf16[64,2,16,64]{0,1,3,2:T(2,128)(2,1)S(1)} %bitcast.149) | data formatting | bytes 786432 | tf_op jit(solution)/shard_map/convert_element_type | solution.py:43
  100.4 9.6 %all-to-all-start.2 = ((bf16[16,2,4096]{2,1,0:T(2,128)(2,1)}), bf16[16,2,4096]{2,1,0:T(2,128)(2,1)S(1)}, u32[]{:S(2)}, u32[]{:S(2)}) async-start(bf16[16,2,4096]{2,1,0:T(2,128)(2,1)} %reshape.87), calls=%async_computation.2 | async-start | bytes 524288 | tf_op jit(solution)/shard_map/all_to_all | solution.py:35
  110.0 16.6 %fusion.20 = f32[16,64,2]{2,1,0:T(8,128)S(1)} fusion(f32[64,2,16,64]{1,0,3,2:T(8,128)} %copy.45, bf16[64,2,16,64]{1,0,3,2:T(8,128)(2,1)} %copy.42), kind=kLoop, calls=%fused_computation.20 | loop fusion | flops 391168 | bytes 794624 | tf_op jit(solution)/shard_map/reduce_sum | solution.py:44
  132.2 488.8 %while.19 = (s32[]{:T(128)}, bf16[1024,2,1,64]{0,3,1,2:T(8,128)(2,1)}, bf16[1024,2,1,64]{0,3,1,2:T(8,128)(2,1)}, f32[1024,2,1,64]{0,3,1,2:T(8,128)S(1)}, f32[102...) while((s32[]{:T(128)}, ...), condition=%wide.region_2.0_spmd.clone, body=%wide.region_1.0_spmd.clone.sunk | while | flops 1361575936 | bytes 66871608 | solution.py:76
  149.7 10.5 %collective-permute-done = bf16[1024,2,1,64]{0,3,1,2:T(8,128)(2,1)} collective-permute-done((bf16[1024,2,1,64]{0,3,1,2:T(8,128)(2,1)S(1)}, bf16[1024,2,1,64]{0,3,1,2:T(8,128)(2,1)}, u32[]{:S(2)}, u32[]{:S(2)}) %collective-permute-start) | collective-permute-done | bytes 262176 | tf_op jit(solution)/shard_map/while/body/eval_jaxpr/ppermute | solution.py:10
  179.0 11.7 %collective-permute-done = bf16[1024,2,1,64]{0,3,1,2:T(8,128)(2,1)} collective-permute-done((bf16[1024,2,1,64]{0,3,1,2:T(8,128)(2,1)S(1)}, bf16[1024,2,1,64]{0,3,1,2:T(8,128)(2,1)}, u32[]{:S(2)}, u32[]{:S(2)}) %collective-permute-start) | collective-permute-done | bytes 262176 | tf_op jit(solution)/shard_map/while/body/eval_jaxpr/ppermute | solution.py:10
  208.3 12.9 %collective-permute-done = bf16[1024,2,1,64]{0,3,1,2:T(8,128)(2,1)} collective-permute-done((bf16[1024,2,1,64]{0,3,1,2:T(8,128)(2,1)S(1)}, bf16[1024,2,1,64]{0,3,1,2:T(8,128)(2,1)}, u32[]{:S(2)}, u32[]{:S(2)}) %collective-permute-start) | collective-permute-done | bytes 262176 | tf_op jit(solution)/shard_map/while/body/eval_jaxpr/ppermute | solution.py:10
  234.6 3.6 fusion.50
  238.3 13.5 %collective-permute-done = bf16[1024,2,1,64]{0,3,1,2:T(8,128)(2,1)} collective-permute-done((bf16[1024,2,1,64]{0,3,1,2:T(8,128)(2,1)S(1)}, bf16[1024,2,1,64]{0,3,1,2:T(8,128)(2,1)}, u32[]{:S(2)}, u32[]{:S(2)}) %collective-permute-start) | collective-permute-done | bytes 262176 | tf_op jit(solution)/shard_map/while/body/eval_jaxpr/ppermute | solution.py:10
  268.8 13.5 %collective-permute-done = bf16[1024,2,1,64]{0,3,1,2:T(8,128)(2,1)} collective-permute-done((bf16[1024,2,1,64]{0,3,1,2:T(8,128)(2,1)S(1)}, bf16[1024,2,1,64]{0,3,1,2:T(8,128)(2,1)}, u32[]{:S(2)}, u32[]{:S(2)}) %collective-permute-start) | collective-permute-done | bytes 262176 | tf_op jit(solution)/shard_map/while/body/eval_jaxpr/ppermute | solution.py:10
  299.3 13.5 %collective-permute-done = bf16[1024,2,1,64]{0,3,1,2:T(8,128)(2,1)} collective-permute-done((bf16[1024,2,1,64]{0,3,1,2:T(8,128)(2,1)S(1)}, bf16[1024,2,1,64]{0,3,1,2:T(8,128)(2,1)}, u32[]{:S(2)}, u32[]{:S(2)}) %collective-permute-start) | collective-permute-done | bytes 262176 | tf_op jit(solution)/shard_map/while/body/eval_jaxpr/ppermute | solution.py:10
  329.9 13.5 %collective-permute-done = bf16[1024,2,1,64]{0,3,1,2:T(8,128)(2,1)} collective-permute-done((bf16[1024,2,1,64]{0,3,1,2:T(8,128)(2,1)S(1)}, bf16[1024,2,1,64]{0,3,1,2:T(8,128)(2,1)}, u32[]{:S(2)}, u32[]{:S(2)}) %collective-permute-start) | collective-permute-done | bytes 262176 | tf_op jit(solution)/shard_map/while/body/eval_jaxpr/ppermute | solution.py:10
  360.4 13.5 %collective-permute-done = bf16[1024,2,1,64]{0,3,1,2:T(8,128)(2,1)} collective-permute-done((bf16[1024,2,1,64]{0,3,1,2:T(8,128)(2,1)S(1)}, bf16[1024,2,1,64]{0,3,1,2:T(8,128)(2,1)}, u32[]{:S(2)}, u32[]{:S(2)}) %collective-permute-start) | collective-permute-done | bytes 262176 | tf_op jit(solution)/shard_map/while/body/eval_jaxpr/ppermute | solution.py:10
  390.9 13.5 %collective-permute-done = bf16[1024,2,1,64]{0,3,1,2:T(8,128)(2,1)} collective-permute-done((bf16[1024,2,1,64]{0,3,1,2:T(8,128)(2,1)S(1)}, bf16[1024,2,1,64]{0,3,1,2:T(8,128)(2,1)}, u32[]{:S(2)}, u32[]{:S(2)}) %collective-permute-start) | collective-permute-done | bytes 262176 | tf_op jit(solution)/shard_map/while/body/eval_jaxpr/ppermute | solution.py:10
  421.5 13.5 %collective-permute-done = bf16[1024,2,1,64]{0,3,1,2:T(8,128)(2,1)} collective-permute-done((bf16[1024,2,1,64]{0,3,1,2:T(8,128)(2,1)S(1)}, bf16[1024,2,1,64]{0,3,1,2:T(8,128)(2,1)}, u32[]{:S(2)}, u32[]{:S(2)}) %collective-permute-start) | collective-permute-done | bytes 262176 | tf_op jit(solution)/shard_map/while/body/eval_jaxpr/ppermute | solution.py:10
  452.0 13.5 %collective-permute-done = bf16[1024,2,1,64]{0,3,1,2:T(8,128)(2,1)} collective-permute-done((bf16[1024,2,1,64]{0,3,1,2:T(8,128)(2,1)S(1)}, bf16[1024,2,1,64]{0,3,1,2:T(8,128)(2,1)}, u32[]{:S(2)}, u32[]{:S(2)}) %collective-permute-start) | collective-permute-done | bytes 262176 | tf_op jit(solution)/shard_map/while/body/eval_jaxpr/ppermute | solution.py:10
  482.6 13.5 %collective-permute-done = bf16[1024,2,1,64]{0,3,1,2:T(8,128)(2,1)} collective-permute-done((bf16[1024,2,1,64]{0,3,1,2:T(8,128)(2,1)S(1)}, bf16[1024,2,1,64]{0,3,1,2:T(8,128)(2,1)}, u32[]{:S(2)}, u32[]{:S(2)}) %collective-permute-start) | collective-permute-done | bytes 262176 | tf_op jit(solution)/shard_map/while/body/eval_jaxpr/ppermute | solution.py:10
  513.1 13.5 %collective-permute-done = bf16[1024,2,1,64]{0,3,1,2:T(8,128)(2,1)} collective-permute-done((bf16[1024,2,1,64]{0,3,1,2:T(8,128)(2,1)S(1)}, bf16[1024,2,1,64]{0,3,1,2:T(8,128)(2,1)}, u32[]{:S(2)}, u32[]{:S(2)}) %collective-permute-start) | collective-permute-done | bytes 262176 | tf_op jit(solution)/shard_map/while/body/eval_jaxpr/ppermute | solution.py:10
  543.6 13.5 %collective-permute-done = bf16[1024,2,1,64]{0,3,1,2:T(8,128)(2,1)} collective-permute-done((bf16[1024,2,1,64]{0,3,1,2:T(8,128)(2,1)S(1)}, bf16[1024,2,1,64]{0,3,1,2:T(8,128)(2,1)}, u32[]{:S(2)}, u32[]{:S(2)}) %collective-permute-start) | collective-permute-done | bytes 262176 | tf_op jit(solution)/shard_map/while/body/eval_jaxpr/ppermute | solution.py:10
  574.2 13.5 %collective-permute-done = bf16[1024,2,1,64]{0,3,1,2:T(8,128)(2,1)} collective-permute-done((bf16[1024,2,1,64]{0,3,1,2:T(8,128)(2,1)S(1)}, bf16[1024,2,1,64]{0,3,1,2:T(8,128)(2,1)}, u32[]{:S(2)}, u32[]{:S(2)}) %collective-permute-start) | collective-permute-done | bytes 262176 | tf_op jit(solution)/shard_map/while/body/eval_jaxpr/ppermute | solution.py:10
  604.7 13.5 %collective-permute-done = bf16[1024,2,1,64]{0,3,1,2:T(8,128)(2,1)} collective-permute-done((bf16[1024,2,1,64]{0,3,1,2:T(8,128)(2,1)S(1)}, bf16[1024,2,1,64]{0,3,1,2:T(8,128)(2,1)}, u32[]{:S(2)}, u32[]{:S(2)}) %collective-permute-start) | collective-permute-done | bytes 262176 | tf_op jit(solution)/shard_map/while/body/eval_jaxpr/ppermute | solution.py:10
  622.6 9.6 %all-to-all-start.6 = ((bf16[16,2,4096]{2,1,0:T(2,128)(2,1)}), bf16[16,2,4096]{2,1,0:T(2,128)(2,1)S(1)}, u32[]{:S(2)}, u32[]{:S(2)}) async-start(bf16[16,2,4096]{2,1,0:T(2,128)(2,1)} %reshape.95), calls=%async_computation.6 | async-start | bytes 524288 | tf_op jit(solution)/shard_map/all_to_all | solution.py:83
  633.8 10.1 %all-to-all-done.6 = bf16[16,2,4096]{2,1,0:T(2,128)(2,1)S(1)} async-done(((bf16[16,2,4096]{2,1,0:T(2,128)(2,1)}), bf16[16,2,4096]{2,1,0:T(2,128)(2,1)S(1)}, u32[]{:S(2)}, u32[]{:S(2)}) %all-to-all-start.6) | async-done | bytes 262176 | tf_op jit(solution)/shard_map/all_to_all | solution.py:83
  648.9 10.0 %all-to-all-done.7 = bf16[16,2,4096]{2,1,0:T(2,128)(2,1)S(1)} async-done(((bf16[16,2,4096]{2,1,0:T(2,128)(2,1)}), bf16[16,2,4096]{2,1,0:T(2,128)(2,1)S(1)}, u32[]{:S(2)}, u32[]{:S(2)}) %all-to-all-start.7) | async-done | bytes 262176 | tf_op jit(solution)/shard_map/all_to_all | solution.py:84
  659.0 3.8 all-to-all-start.8
  666.7 7.4 %all-to-all-done.8 = bf16[16,2,4096]{2,1,0:T(2,128)(2,1)S(1)} async-done(((bf16[16,2,4096]{2,1,0:T(2,128)(2,1)}), bf16[16,2,4096]{2,1,0:T(2,128)(2,1)S(1)}, u32[]{:S(2)}, u32[]{:S(2)}) %all-to-all-start.8) | async-done | bytes 262176 | tf_op jit(solution)/shard_map/all_to_all | solution.py:85
  (315 shorter events, 322.2 us)
Async XLA Ops:
  67.8 32.6 %all-to-all-start.1 = ((bf16[16,2,4096]{2,1,0:T(2,128)(2,1)}), bf16[16,2,4096]{2,1,0:T(2,128)(2,1)S(1)}, u32[]{:S(2)}, u32[]{:S(2)}) async-start(bf16[16,2,4096]{2,1,0:T(2,128)(2,1)} %reshape.85), calls=%async_computation.1 | async-start | bytes 524288 | tf_op jit(solution)/shard_map/all_to_all | solution.py:37
  100.4 30.6 %all-to-all-start.2 = ((bf16[16,2,4096]{2,1,0:T(2,128)(2,1)}), bf16[16,2,4096]{2,1,0:T(2,128)(2,1)S(1)}, u32[]{:S(2)}, u32[]{:S(2)}) async-start(bf16[16,2,4096]{2,1,0:T(2,128)(2,1)} %reshape.87), calls=%async_computation.2 | async-start | bytes 524288 | tf_op jit(solution)/shard_map/all_to_all | solution.py:35
  140.8 22.1 %collective-permute-start.2 = (f32[1024,2,1,64]{0,3,1,2:T(8,128)S(1)}, f32[1024,2,1,64]{0,3,1,2:T(8,128)S(1)}, u32[]{:S(2)}, u32[]{:S(2)}) collective-permute-start(f32[1024,2,1,64]{0,3,1,2:T(8,128)S(1)} %fusion.48), channel_id=1, source_target_pairs={{240,0},{0,16},{16,32},{32,48},{48,64},{64,80},{80,96},{96,112},{1... | collective-permute-start | bytes 1572872 | tf_op jit(solution)/shard_map/while/body/eval_jaxpr/ppermute | solution.py:10
  142.7 20.2 %collective-permute-start.3 = (f32[1024,2,1,64]{0,3,1,2:T(8,128)S(1)}, f32[1024,2,1,64]{0,3,1,2:T(8,128)S(1)}, u32[]{:S(2)}, u32[]{:S(2)}) collective-permute-start(f32[1024,2,1,64]{0,3,1,2:T(8,128)S(1)} %fusion.49), channel_id=1, source_target_pairs={{240,0},{0,16},{16,32},{32,48},{48,64},{64,80},{80,96},{96,112},{1... | collective-permute-start | bytes 1572872 | tf_op jit(solution)/shard_map/while/body/eval_jaxpr/ppermute | solution.py:10
  171.4 22.1 %collective-permute-start.2 = (f32[1024,2,1,64]{0,3,1,2:T(8,128)S(1)}, f32[1024,2,1,64]{0,3,1,2:T(8,128)S(1)}, u32[]{:S(2)}, u32[]{:S(2)}) collective-permute-start(f32[1024,2,1,64]{0,3,1,2:T(8,128)S(1)} %fusion.48), channel_id=1, source_target_pairs={{240,0},{0,16},{16,32},{32,48},{48,64},{64,80},{80,96},{96,112},{1... | collective-permute-start | bytes 1572872 | tf_op jit(solution)/shard_map/while/body/eval_jaxpr/ppermute | solution.py:10
  173.3 20.2 %collective-permute-start.3 = (f32[1024,2,1,64]{0,3,1,2:T(8,128)S(1)}, f32[1024,2,1,64]{0,3,1,2:T(8,128)S(1)}, u32[]{:S(2)}, u32[]{:S(2)}) collective-permute-start(f32[1024,2,1,64]{0,3,1,2:T(8,128)S(1)} %fusion.49), channel_id=1, source_target_pairs={{240,0},{0,16},{16,32},{32,48},{48,64},{64,80},{80,96},{96,112},{1... | collective-permute-start | bytes 1572872 | tf_op jit(solution)/shard_map/while/body/eval_jaxpr/ppermute | solution.py:10
  201.9 22.1 %collective-permute-start.2 = (f32[1024,2,1,64]{0,3,1,2:T(8,128)S(1)}, f32[1024,2,1,64]{0,3,1,2:T(8,128)S(1)}, u32[]{:S(2)}, u32[]{:S(2)}) collective-permute-start(f32[1024,2,1,64]{0,3,1,2:T(8,128)S(1)} %fusion.48), channel_id=1, source_target_pairs={{240,0},{0,16},{16,32},{32,48},{48,64},{64,80},{80,96},{96,112},{1... | collective-permute-start | bytes 1572872 | tf_op jit(solution)/shard_map/while/body/eval_jaxpr/ppermute | solution.py:10
  203.8 20.2 %collective-permute-start.3 = (f32[1024,2,1,64]{0,3,1,2:T(8,128)S(1)}, f32[1024,2,1,64]{0,3,1,2:T(8,128)S(1)}, u32[]{:S(2)}, u32[]{:S(2)}) collective-permute-start(f32[1024,2,1,64]{0,3,1,2:T(8,128)S(1)} %fusion.49), channel_id=1, source_target_pairs={{240,0},{0,16},{16,32},{32,48},{48,64},{64,80},{80,96},{96,112},{1... | collective-permute-start | bytes 1572872 | tf_op jit(solution)/shard_map/while/body/eval_jaxpr/ppermute | solution.py:10
  232.4 22.1 %collective-permute-start.2 = (f32[1024,2,1,64]{0,3,1,2:T(8,128)S(1)}, f32[1024,2,1,64]{0,3,1,2:T(8,128)S(1)}, u32[]{:S(2)}, u32[]{:S(2)}) collective-permute-start(f32[1024,2,1,64]{0,3,1,2:T(8,128)S(1)} %fusion.48), channel_id=1, source_target_pairs={{240,0},{0,16},{16,32},{32,48},{48,64},{64,80},{80,96},{96,112},{1... | collective-permute-start | bytes 1572872 | tf_op jit(solution)/shard_map/while/body/eval_jaxpr/ppermute | solution.py:10
  234.3 20.2 %collective-permute-start.3 = (f32[1024,2,1,64]{0,3,1,2:T(8,128)S(1)}, f32[1024,2,1,64]{0,3,1,2:T(8,128)S(1)}, u32[]{:S(2)}, u32[]{:S(2)}) collective-permute-start(f32[1024,2,1,64]{0,3,1,2:T(8,128)S(1)} %fusion.49), channel_id=1, source_target_pairs={{240,0},{0,16},{16,32},{32,48},{48,64},{64,80},{80,96},{96,112},{1... | collective-permute-start | bytes 1572872 | tf_op jit(solution)/shard_map/while/body/eval_jaxpr/ppermute | solution.py:10
  263.0 22.1 %collective-permute-start.2 = (f32[1024,2,1,64]{0,3,1,2:T(8,128)S(1)}, f32[1024,2,1,64]{0,3,1,2:T(8,128)S(1)}, u32[]{:S(2)}, u32[]{:S(2)}) collective-permute-start(f32[1024,2,1,64]{0,3,1,2:T(8,128)S(1)} %fusion.48), channel_id=1, source_target_pairs={{240,0},{0,16},{16,32},{32,48},{48,64},{64,80},{80,96},{96,112},{1... | collective-permute-start | bytes 1572872 | tf_op jit(solution)/shard_map/while/body/eval_jaxpr/ppermute | solution.py:10
  264.9 20.2 %collective-permute-start.3 = (f32[1024,2,1,64]{0,3,1,2:T(8,128)S(1)}, f32[1024,2,1,64]{0,3,1,2:T(8,128)S(1)}, u32[]{:S(2)}, u32[]{:S(2)}) collective-permute-start(f32[1024,2,1,64]{0,3,1,2:T(8,128)S(1)} %fusion.49), channel_id=1, source_target_pairs={{240,0},{0,16},{16,32},{32,48},{48,64},{64,80},{80,96},{96,112},{1... | collective-permute-start | bytes 1572872 | tf_op jit(solution)/shard_map/while/body/eval_jaxpr/ppermute | solution.py:10
  293.5 22.1 %collective-permute-start.2 = (f32[1024,2,1,64]{0,3,1,2:T(8,128)S(1)}, f32[1024,2,1,64]{0,3,1,2:T(8,128)S(1)}, u32[]{:S(2)}, u32[]{:S(2)}) collective-permute-start(f32[1024,2,1,64]{0,3,1,2:T(8,128)S(1)} %fusion.48), channel_id=1, source_target_pairs={{240,0},{0,16},{16,32},{32,48},{48,64},{64,80},{80,96},{96,112},{1... | collective-permute-start | bytes 1572872 | tf_op jit(solution)/shard_map/while/body/eval_jaxpr/ppermute | solution.py:10
  295.4 20.2 %collective-permute-start.3 = (f32[1024,2,1,64]{0,3,1,2:T(8,128)S(1)}, f32[1024,2,1,64]{0,3,1,2:T(8,128)S(1)}, u32[]{:S(2)}, u32[]{:S(2)}) collective-permute-start(f32[1024,2,1,64]{0,3,1,2:T(8,128)S(1)} %fusion.49), channel_id=1, source_target_pairs={{240,0},{0,16},{16,32},{32,48},{48,64},{64,80},{80,96},{96,112},{1... | collective-permute-start | bytes 1572872 | tf_op jit(solution)/shard_map/while/body/eval_jaxpr/ppermute | solution.py:10
  324.0 22.1 %collective-permute-start.2 = (f32[1024,2,1,64]{0,3,1,2:T(8,128)S(1)}, f32[1024,2,1,64]{0,3,1,2:T(8,128)S(1)}, u32[]{:S(2)}, u32[]{:S(2)}) collective-permute-start(f32[1024,2,1,64]{0,3,1,2:T(8,128)S(1)} %fusion.48), channel_id=1, source_target_pairs={{240,0},{0,16},{16,32},{32,48},{48,64},{64,80},{80,96},{96,112},{1... | collective-permute-start | bytes 1572872 | tf_op jit(solution)/shard_map/while/body/eval_jaxpr/ppermute | solution.py:10
  325.9 20.2 %collective-permute-start.3 = (f32[1024,2,1,64]{0,3,1,2:T(8,128)S(1)}, f32[1024,2,1,64]{0,3,1,2:T(8,128)S(1)}, u32[]{:S(2)}, u32[]{:S(2)}) collective-permute-start(f32[1024,2,1,64]{0,3,1,2:T(8,128)S(1)} %fusion.49), channel_id=1, source_target_pairs={{240,0},{0,16},{16,32},{32,48},{48,64},{64,80},{80,96},{96,112},{1... | collective-permute-start | bytes 1572872 | tf_op jit(solution)/shard_map/while/body/eval_jaxpr/ppermute | solution.py:10
  354.6 22.1 %collective-permute-start.2 = (f32[1024,2,1,64]{0,3,1,2:T(8,128)S(1)}, f32[1024,2,1,64]{0,3,1,2:T(8,128)S(1)}, u32[]{:S(2)}, u32[]{:S(2)}) collective-permute-start(f32[1024,2,1,64]{0,3,1,2:T(8,128)S(1)} %fusion.48), channel_id=1, source_target_pairs={{240,0},{0,16},{16,32},{32,48},{48,64},{64,80},{80,96},{96,112},{1... | collective-permute-start | bytes 1572872 | tf_op jit(solution)/shard_map/while/body/eval_jaxpr/ppermute | solution.py:10
  356.5 20.2 %collective-permute-start.3 = (f32[1024,2,1,64]{0,3,1,2:T(8,128)S(1)}, f32[1024,2,1,64]{0,3,1,2:T(8,128)S(1)}, u32[]{:S(2)}, u32[]{:S(2)}) collective-permute-start(f32[1024,2,1,64]{0,3,1,2:T(8,128)S(1)} %fusion.49), channel_id=1, source_target_pairs={{240,0},{0,16},{16,32},{32,48},{48,64},{64,80},{80,96},{96,112},{1... | collective-permute-start | bytes 1572872 | tf_op jit(solution)/shard_map/while/body/eval_jaxpr/ppermute | solution.py:10
  385.1 22.1 %collective-permute-start.2 = (f32[1024,2,1,64]{0,3,1,2:T(8,128)S(1)}, f32[1024,2,1,64]{0,3,1,2:T(8,128)S(1)}, u32[]{:S(2)}, u32[]{:S(2)}) collective-permute-start(f32[1024,2,1,64]{0,3,1,2:T(8,128)S(1)} %fusion.48), channel_id=1, source_target_pairs={{240,0},{0,16},{16,32},{32,48},{48,64},{64,80},{80,96},{96,112},{1... | collective-permute-start | bytes 1572872 | tf_op jit(solution)/shard_map/while/body/eval_jaxpr/ppermute | solution.py:10
  415.7 22.1 %collective-permute-start.2 = (f32[1024,2,1,64]{0,3,1,2:T(8,128)S(1)}, f32[1024,2,1,64]{0,3,1,2:T(8,128)S(1)}, u32[]{:S(2)}, u32[]{:S(2)}) collective-permute-start(f32[1024,2,1,64]{0,3,1,2:T(8,128)S(1)} %fusion.48), channel_id=1, source_target_pairs={{240,0},{0,16},{16,32},{32,48},{48,64},{64,80},{80,96},{96,112},{1... | collective-permute-start | bytes 1572872 | tf_op jit(solution)/shard_map/while/body/eval_jaxpr/ppermute | solution.py:10
  417.6 20.2 %collective-permute-start.3 = (f32[1024,2,1,64]{0,3,1,2:T(8,128)S(1)}, f32[1024,2,1,64]{0,3,1,2:T(8,128)S(1)}, u32[]{:S(2)}, u32[]{:S(2)}) collective-permute-start(f32[1024,2,1,64]{0,3,1,2:T(8,128)S(1)} %fusion.49), channel_id=1, source_target_pairs={{240,0},{0,16},{16,32},{32,48},{48,64},{64,80},{80,96},{96,112},{1... | collective-permute-start | bytes 1572872 | tf_op jit(solution)/shard_map/while/body/eval_jaxpr/ppermute | solution.py:10
  446.2 22.1 %collective-permute-start.2 = (f32[1024,2,1,64]{0,3,1,2:T(8,128)S(1)}, f32[1024,2,1,64]{0,3,1,2:T(8,128)S(1)}, u32[]{:S(2)}, u32[]{:S(2)}) collective-permute-start(f32[1024,2,1,64]{0,3,1,2:T(8,128)S(1)} %fusion.48), channel_id=1, source_target_pairs={{240,0},{0,16},{16,32},{32,48},{48,64},{64,80},{80,96},{96,112},{1... | collective-permute-start | bytes 1572872 | tf_op jit(solution)/shard_map/while/body/eval_jaxpr/ppermute | solution.py:10
  448.1 20.2 %collective-permute-start.3 = (f32[1024,2,1,64]{0,3,1,2:T(8,128)S(1)}, f32[1024,2,1,64]{0,3,1,2:T(8,128)S(1)}, u32[]{:S(2)}, u32[]{:S(2)}) collective-permute-start(f32[1024,2,1,64]{0,3,1,2:T(8,128)S(1)} %fusion.49), channel_id=1, source_target_pairs={{240,0},{0,16},{16,32},{32,48},{48,64},{64,80},{80,96},{96,112},{1... | collective-permute-start | bytes 1572872 | tf_op jit(solution)/shard_map/while/body/eval_jaxpr/ppermute | solution.py:10
  476.7 22.1 %collective-permute-start.2 = (f32[1024,2,1,64]{0,3,1,2:T(8,128)S(1)}, f32[1024,2,1,64]{0,3,1,2:T(8,128)S(1)}, u32[]{:S(2)}, u32[]{:S(2)}) collective-permute-start(f32[1024,2,1,64]{0,3,1,2:T(8,128)S(1)} %fusion.48), channel_id=1, source_target_pairs={{240,0},{0,16},{16,32},{32,48},{48,64},{64,80},{80,96},{96,112},{1... | collective-permute-start | bytes 1572872 | tf_op jit(solution)/shard_map/while/body/eval_jaxpr/ppermute | solution.py:10
  507.3 22.1 %collective-permute-start.2 = (f32[1024,2,1,64]{0,3,1,2:T(8,128)S(1)}, f32[1024,2,1,64]{0,3,1,2:T(8,128)S(1)}, u32[]{:S(2)}, u32[]{:S(2)}) collective-permute-start(f32[1024,2,1,64]{0,3,1,2:T(8,128)S(1)} %fusion.48), channel_id=1, source_target_pairs={{240,0},{0,16},{16,32},{32,48},{48,64},{64,80},{80,96},{96,112},{1... | collective-permute-start | bytes 1572872 | tf_op jit(solution)/shard_map/while/body/eval_jaxpr/ppermute | solution.py:10
  509.2 20.2 %collective-permute-start.3 = (f32[1024,2,1,64]{0,3,1,2:T(8,128)S(1)}, f32[1024,2,1,64]{0,3,1,2:T(8,128)S(1)}, u32[]{:S(2)}, u32[]{:S(2)}) collective-permute-start(f32[1024,2,1,64]{0,3,1,2:T(8,128)S(1)} %fusion.49), channel_id=1, source_target_pairs={{240,0},{0,16},{16,32},{32,48},{48,64},{64,80},{80,96},{96,112},{1... | collective-permute-start | bytes 1572872 | tf_op jit(solution)/shard_map/while/body/eval_jaxpr/ppermute | solution.py:10
  537.8 22.1 %collective-permute-start.2 = (f32[1024,2,1,64]{0,3,1,2:T(8,128)S(1)}, f32[1024,2,1,64]{0,3,1,2:T(8,128)S(1)}, u32[]{:S(2)}, u32[]{:S(2)}) collective-permute-start(f32[1024,2,1,64]{0,3,1,2:T(8,128)S(1)} %fusion.48), channel_id=1, source_target_pairs={{240,0},{0,16},{16,32},{32,48},{48,64},{64,80},{80,96},{96,112},{1... | collective-permute-start | bytes 1572872 | tf_op jit(solution)/shard_map/while/body/eval_jaxpr/ppermute | solution.py:10
  539.7 20.2 %collective-permute-start.3 = (f32[1024,2,1,64]{0,3,1,2:T(8,128)S(1)}, f32[1024,2,1,64]{0,3,1,2:T(8,128)S(1)}, u32[]{:S(2)}, u32[]{:S(2)}) collective-permute-start(f32[1024,2,1,64]{0,3,1,2:T(8,128)S(1)} %fusion.49), channel_id=1, source_target_pairs={{240,0},{0,16},{16,32},{32,48},{48,64},{64,80},{80,96},{96,112},{1... | collective-permute-start | bytes 1572872 | tf_op jit(solution)/shard_map/while/body/eval_jaxpr/ppermute | solution.py:10
  568.3 22.1 %collective-permute-start.2 = (f32[1024,2,1,64]{0,3,1,2:T(8,128)S(1)}, f32[1024,2,1,64]{0,3,1,2:T(8,128)S(1)}, u32[]{:S(2)}, u32[]{:S(2)}) collective-permute-start(f32[1024,2,1,64]{0,3,1,2:T(8,128)S(1)} %fusion.48), channel_id=1, source_target_pairs={{240,0},{0,16},{16,32},{32,48},{48,64},{64,80},{80,96},{96,112},{1... | collective-permute-start | bytes 1572872 | tf_op jit(solution)/shard_map/while/body/eval_jaxpr/ppermute | solution.py:10
  598.9 22.1 %collective-permute-start.2 = (f32[1024,2,1,64]{0,3,1,2:T(8,128)S(1)}, f32[1024,2,1,64]{0,3,1,2:T(8,128)S(1)}, u32[]{:S(2)}, u32[]{:S(2)}) collective-permute-start(f32[1024,2,1,64]{0,3,1,2:T(8,128)S(1)} %fusion.48), channel_id=1, source_target_pairs={{240,0},{0,16},{16,32},{32,48},{48,64},{64,80},{80,96},{96,112},{1... | collective-permute-start | bytes 1572872 | tf_op jit(solution)/shard_map/while/body/eval_jaxpr/ppermute | solution.py:10
  600.8 20.2 %collective-permute-start.3 = (f32[1024,2,1,64]{0,3,1,2:T(8,128)S(1)}, f32[1024,2,1,64]{0,3,1,2:T(8,128)S(1)}, u32[]{:S(2)}, u32[]{:S(2)}) collective-permute-start(f32[1024,2,1,64]{0,3,1,2:T(8,128)S(1)} %fusion.49), channel_id=1, source_target_pairs={{240,0},{0,16},{16,32},{32,48},{48,64},{64,80},{80,96},{96,112},{1... | collective-permute-start | bytes 1572872 | tf_op jit(solution)/shard_map/while/body/eval_jaxpr/ppermute | solution.py:10
  622.6 21.3 %all-to-all-start.6 = ((bf16[16,2,4096]{2,1,0:T(2,128)(2,1)}), bf16[16,2,4096]{2,1,0:T(2,128)(2,1)S(1)}, u32[]{:S(2)}, u32[]{:S(2)}) async-start(bf16[16,2,4096]{2,1,0:T(2,128)(2,1)} %reshape.95), calls=%async_computation.6 | async-start | bytes 524288 | tf_op jit(solution)/shard_map/all_to_all | solution.py:83
  (58 other events, 867.4 us)
where the time goes:
time: 679 us; the launch traced here: 676 us
  waiting for transfers between devices  319 us (47%)
  matrix products  179 us (26%)
  local copies, waits for them, and re-layouts  97.8 us (14%)
  starting transfers between devices  60.8 us (9%)
  other arithmetic  17.5 us (3%)
    ppermute x64, waiting for transfers between devices, shifted(): return lax.ppermute(block, axis, route)  255 us
    dot_general x16, matrix products, cycle_turn(): jnp.einsum('hsqk,kshd->qshd', grad_scores, keys_now, preferred_element_ty...  58.2 us
    dot_general x16, matrix products, block_terms(): jnp.einsum('qshd,kshd->hsqk', grad_rows, values_blk, preferred_element_ty...  57.8 us
    while x64, local copies, waits for them, and re-layouts  42 us
    dot_general x16, matrix products, cycle_turn(): jnp.einsum('hsqk,qshd->kshd', attn_probs.astype(jnp.bfloat16), grad_rows,...  28.8 us
    dot_general x16, matrix products, block_terms(): jnp.einsum('qshd,kshd->hsqk', queries, keys_blk, preferred_element_type=j...  20.7 us
    unnamed x28, local copies, waits for them, and re-layouts  20.5 us
    reduce_sum x1, other arithmetic, shards(): jnp.sum(products.reshape(block_rows, seq_count, head_local, head_size), a...  16.6 us
  transfers between devices with their start and end apart: 73, of which 39 were waited for; matrix products, arithmetic and copies ran while one was open for 22% of the time, Pallas kernels for 0%

commit v1 on v0

v1 whole, which is shorter than its diff:
```python
import math
import jax
import jax.numpy as jnp
from jax import lax
from jax.experimental import pallas as pl
from jax.experimental.pallas import tpu as pltpu
from jax.sharding import PartitionSpec as P

BF, F32 = jnp.bfloat16, jnp.float32
MESH = pl.DeviceIdType.MESH
NT = (((1,), (1,)), ((), ()))
TN = (((0,), (0,)), ((), ()))
LOG2E = math.log2(math.e)
SCALE = 0.125
ROWS = 1024
SLOT = 64


def iota(shape, dim):
    return lax.broadcasted_iota(jnp.int32, shape, dim)


def low_half(rows):
    return iota((rows, 128), 1) < 64


def roll_half(tile):
    return pltpu.roll(tile, 64, 1)


def order_rows(transposed):
    shape = (128, 128)
    here, there = (iota(shape, 1), iota(shape, 0)) if transposed else (iota(shape, 0), iota(shape, 1))
    return jnp.where(there == 2 * lax.rem(here, 64) + lax.div(here, 64), 1.0, 0.0).astype(BF)


def place(high):
    return jnp.where(iota((64, 128), 1) == iota((64, 128), 0) + (64 if high else 0), 1.0, 0.0).astype(BF)


def kernel(
    q_ref, k_ref, v_ref, o_ref, g_ref, lse_ref, dq_ref, dk_ref, dv_ref,
    sq, sk, sa, qbuf, kbuf, ra, aux, kz, vz, kt, dqt, dka, dva,
    sdq, rdq, skv, rkv, oq, okv, iq, ikv,
    in_send, in_recv, ag_send, ag_recv, ax_send, ax_recv, dq_send, dq_recv,
    kx_send, kx_recv, dx_send, dx_recv, out_send, out_recv,
):
    blk, head = lax.axis_index("blk"), lax.axis_index("head")
    my_y, my_zl, my_c = lax.div(blk, 4), lax.rem(lax.div(blk, 2), 2), lax.rem(blk, 2)
    my_x, my_zh = lax.div(head, 4), lax.rem(head, 4)
    my_pair = my_x * 8 + my_y * 2 + my_zl

    def device(x, y, zl, zh, c):
        return (y * 4 + zl * 2 + c, x * 4 + zh)

    def offset(n):
        oy = lax.rem(lax.div(n, 2), 4)
        return lax.rem(lax.div(n, 8) + oy, 4), oy, lax.rem(n, 2)

    def ahead(n):
        ox, oy, ol = offset(n)
        return lax.rem(my_x + ox, 4), lax.rem(my_y + oy, 4), lax.rem(my_zl + ol, 2)

    def behind(n):
        ox, oy, ol = offset(n)
        return lax.rem(my_x + 4 - ox, 4), lax.rem(my_y + 4 - oy, 4), lax.rem(my_zl + 2 - ol, 2)

    def ring(distance):
        return device(my_x, my_y, my_zl, lax.rem(my_zh + distance, 4), my_c)

    partner = device(my_x, my_y, my_zl, my_zh, 1 - my_c)

    def send(src, dst, send_sem, recv_sem, target):
        return pltpu.make_async_remote_copy(
            src_ref=src, dst_ref=dst, send_sem=send_sem, recv_sem=recv_sem, device_id=target, device_id_type=MESH
        )

    def wait(ref, sem):
        pltpu.make_async_copy(ref, ref, sem).wait()

    barrier = pltpu.get_barrier_semaphore()

    def greet(n, c):
        x, y, zl = ahead(n)
        pl.semaphore_signal(barrier, inc=1, device_id=device(x, y, zl, my_zh, my_c), device_id_type=MESH)
        return c

    lax.fori_loop(1, 32, greet, 0)
    for target in (partner, ring(1), ring(2), ring(3)):
        pl.semaphore_signal(barrier, inc=1, device_id=target, device_id_type=MESH)

    to_seq = order_rows(False)

    def by_seq(ref):
        return jnp.dot(to_seq, ref[...], preferred_element_type=F32)

    def pack(low, high, dst):
        for t in range(8):
            a, b = low[:, t * 128:(t + 1) * 128], high[:, t * 128:(t + 1) * 128]
            even = jnp.where(low_half(128), a, roll_half(b)).astype(BF)
            odd = jnp.where(low_half(128), roll_half(a), b).astype(BF)
            for s in range(2):
                dst[4 * t + s] = even[s * 64:(s + 1) * 64]
                dst[4 * t + 2 + s] = odd[s * 64:(s + 1) * 64]

    grad_rows = by_seq(g_ref)
    pack(by_seq(q_ref), grad_rows, sq)
    rest = by_seq(o_ref) * grad_rows
    heads_of = jnp.where(iota((16, 1024), 0) == lax.div(iota((16, 1024), 1), 64), 1.0, 0.0).astype(BF)
    dots = jnp.zeros((16, 128), F32)
    for _ in range(3):
        part = rest.astype(BF)
        rest = rest - part.astype(F32)
        dots = dots + lax.dot_general(heads_of, part, NT, preferred_element_type=F32)
    dots_rolled = roll_half(dots)
    for h in range(16):
        for s in range(2):
            sa[2 * h + s, :, 0:64] = lse_ref[h, s:s + 1, :] * LOG2E
            sa[2 * h + s, :, 64:128] = (dots if s else dots_rolled)[h:h + 1, 64:128]
    pl.semaphore_wait(barrier, 35)

    def send_queries(n, c):
        x, y, zl = ahead(n)
        pair, target = x * 8 + y * 2 + zl, device(x, y, zl, my_zh, my_c)
        half, row = lax.div(n, 16), pl.multiple_of(lax.rem(n, 16) * SLOT, SLOT)
        send(sa.at[pair], ra.at[n], in_send.at[0], in_recv.at[half], target).start()
        send(sq.at[pair], qbuf.at[7 * half, pl.ds(row, SLOT)], in_send.at[1], in_recv.at[2 + half], target).start()
        return c

    def send_keys(n, c):
        x, y, zl = ahead(n)
        pair, target = x * 8 + y * 2 + zl, device(x, y, zl, my_zh, my_c)
        half, row = lax.div(n, 16), pl.multiple_of(lax.rem(n, 16) * SLOT, SLOT)
        send(sk.at[pair], kbuf.at[half, pl.ds(row, SLOT)], in_send.at[2], in_recv.at[4 + half], target).start()
        return c

    lax.fori_loop(1, 16, send_queries, 0)
    pack(by_seq(k_ref), by_seq(v_ref), sk)
    lax.fori_loop(1, 32, send_keys, 0)
    lax.fori_loop(16, 32, send_queries, 0)
    ra[0] = sa[my_pair]
    qbuf[0, 0:SLOT] = sq[my_pair]
    kbuf[0, 0:SLOT] = sk[my_pair]
    dqt[...] = jnp.zeros_like(dqt)
    dka[...] = jnp.zeros_like(dka)
    dva[...] = jnp.zeros_like(dva)

    def queries_here(half):
        first = 0 if half else 1
        wait(ra.at[pl.ds(16 * half + first, 16 - first)], in_recv.at[half])
        wait(qbuf.at[7 * half, pl.ds(0, (16 - first) * SLOT)], in_recv.at[2 + half])
        for m in range(8):
            a, b = ra[16 * half + 2 * m], ra[16 * half + 2 * m + 1]
            aux[7 * half, 0:1, m * 128:(m + 1) * 128] = jnp.where(low_half(1), a, roll_half(b))
            aux[7 * half, 1:2, m * 128:(m + 1) * 128] = jnp.where(low_half(1), roll_half(a), b)

    def pass_chunk(src, dst, distance):
        target = ring(distance)
        for buf, ss, rs in ((qbuf, ag_send, ag_recv), (aux, ax_send, ax_recv)):
            send(buf.at[src], buf.at[dst], ss.at[dst], rs.at[dst], target).start()

    def chunk_here(i):
        wait(qbuf.at[i], ag_recv.at[i])
        wait(aux.at[i], ax_recv.at[i])

    def prepare_keys(j):
        both = kbuf[j]
        low = low_half(ROWS)
        zero = jnp.zeros_like(both)
        kz[j] = jnp.where(low, both, zero)
        vz[j] = jnp.where(low, zero, both)
        eye = jnp.where(iota((64, 128), 0) == iota((64, 128), 1), 1.0, 0.0).astype(BF)
        kt[j] = lax.dot_general(eye, both, NT, preferred_element_type=F32).astype(BF)

    def keys_here(j):
        if j < 2:
            first = 0 if j else 1
            wait(kbuf.at[j, pl.ds(0, (16 - first) * SLOT)], in_recv.at[4 + j])
            send(kbuf.at[j], kbuf.at[2 + j], kx_send.at[j], kx_recv.at[j], partner).start()
        else:
            wait(kbuf.at[j], kx_recv.at[j - 2])
        prepare_keys(j)

    def both_grads(j):
        return jnp.where(low_half(ROWS), dka[j] * SCALE, dva[j])

    def send_out(lo, hi, src, dst, which):
        def one(n, c):
            x, y, zl = behind(n)
            target = device(x, y, zl, my_zh, my_c)
            send(src.at[n], dst.at[my_pair], out_send.at[which], out_recv.at[which], target).start()
            return c

        lax.fori_loop(max(lo, 1), hi, one, 0)
        if lo == 0:
            dst[my_pair] = src[0]

    def finish_queries(half):
        parts = (3, 4, 6) if half else (1, 2, 5)
        total = dqt[7 * half]
        for i in parts:
            wait(rdq.at[i - 1], dq_recv.at[i])
            total = total + rdq[i - 1].astype(F32)
        low = (total * SCALE).astype(BF)
        a = lax.dot_general(low, place(False), TN, preferred_element_type=F32)
        b = lax.dot_general(low, place(True), TN, preferred_element_type=F32)
        for n in range(16):
            both = a[n * 64:n * 64 + 32] + b[n * 64 + 32:n * 64 + 64]
            oq[16 * half + n] = both.astype(BF)
        send_out(16 * half, 16 * half + 16, oq, iq, 0)

    def finish_keys(j):
        wait(rkv.at[j], dx_recv.at[j])
        total = (both_grads(j) + rkv[j].astype(F32)).astype(BF)
        for n in range(16):
            okv[16 * j + n] = total[n * 64:(n + 1) * 64]
        send_out(16 * j, 16 * j + 16, okv, ikv, 1)

    queries_here(0)
    pass_chunk(0, 1, 3)
    pass_chunk(0, 2, 1)
    keys_here(0)

    def turn(t, c):
        i = lax.div(t, 4)
        j = lax.rem(lax.rem(t, 4) + 2 * lax.div(i, 7), 4)

        @pl.when(t == 1)
        def _():
            keys_here(1)
            queries_here(1)
            pass_chunk(7, 3, 3)
            pass_chunk(7, 4, 1)

        @pl.when(t == 2)
        def _():
            keys_here(2)

        @pl.when(t == 3)
        def _():
            keys_here(3)

        @pl.when(t == 4)
        def _():
            chunk_here(1)
            pass_chunk(1, 5, 3)

        @pl.when(t == 8)
        def _():
            chunk_here(2)

        @pl.when(t == 12)
        def _():
            chunk_here(3)
            chunk_here(4)
            pass_chunk(4, 6, 1)

        @pl.when(t == 20)
        def _():
            chunk_here(5)

        @pl.when(t == 24)
        def _():
            chunk_here(6)

        @pl.when(t == 30)
        def _():
            finish_queries(0)

        rows = qbuf[i]
        scores = lax.dot_general(kz[j], rows, NT, preferred_element_type=F32)
        grad_probs = lax.dot_general(vz[j], rows, NT, preferred_element_type=F32)
        probs = jnp.exp2(scores * (SCALE * LOG2E) - aux[i, 0:1, :])
        grad_scores = (probs * (grad_probs - aux[i, 1:2, :])).astype(BF)
        dva[j] += jnp.dot(probs.astype(BF), rows, preferred_element_type=F32)
        dka[j] += jnp.dot(grad_scores, rows, preferred_element_type=F32)
        dqt[i] += jnp.dot(kt[j], grad_scores, preferred_element_type=F32)

        for i_done, distance in ((1, 1), (2, 3), (3, 1), (4, 3), (5, 2), (6, 2)):

            @pl.when(t == 4 * i_done + 3)
            def _():
                sdq[i_done - 1] = dqt[i_done].astype(BF)
                send(sdq.at[i_done - 1], rdq.at[i_done - 1], dq_send.at[i_done], dq_recv.at[i_done], ring(distance)).start()

        for half in range(2):

            @pl.when(t == 28 + half)
            def _():
                skv[half] = both_grads(2 + half).astype(BF)
                send(skv.at[half], rkv.at[half], dx_send.at[half], dx_recv.at[half], partner).start()

        @pl.when(t == 30)
        def _():
            finish_keys(0)

        return c

    lax.fori_loop(0, 32, turn, 0)
    finish_keys(1)
    finish_queries(1)

    wait(sa.at[pl.ds(0, 31)], in_send.at[0])
    wait(sq.at[pl.ds(0, 31)], in_send.at[1])
    wait(sk.at[pl.ds(0, 31)], in_send.at[2])
    for i in range(1, 7):
        wait(qbuf.at[i], ag_send.at[i])
        wait(aux.at[i], ax_send.at[i])
        wait(sdq.at[i - 1], dq_send.at[i])
    for j in range(2):
        wait(kbuf.at[j], kx_send.at[j])
        wait(skv.at[j], dx_send.at[j])
    wait(oq.at[pl.ds(0, 31)], out_send.at[0])
    wait(okv.at[pl.ds(0, 31)], out_send.at[1])

    to_frames = order_rows(True)

    def interleave(tiles):
        rows = jnp.concatenate([jnp.concatenate([tiles(s, t) for t in range(8)], 1) for s in range(2)], 0)
        return jnp.dot(to_frames, rows.astype(BF), preferred_element_type=F32).astype(BF)

    wait(ikv.at[pl.ds(0, 31)], out_recv.at[1])

    def key_tile(s, t):
        return jnp.where(low_half(64), ikv[4 * t + s].astype(F32), roll_half(ikv[4 * t + 2 + s].astype(F32)))

    def value_tile(s, t):
        return jnp.where(low_half(64), roll_half(ikv[4 * t + s].astype(F32)), ikv[4 * t + 2 + s].astype(F32))

    def query_tile(s, t):
        a, b = iq[4 * t + s].astype(F32), iq[4 * t + 2 + s].astype(F32)
        first = jnp.where(low_half(32), a, roll_half(b))
        second = jnp.where(low_half(32), roll_half(a), b)
        return jnp.concatenate([first, second], 0)

    dk_ref[...] = interleave(key_tile)
    dv_ref[...] = interleave(value_tile)
    wait(iq.at[pl.ds(0, 31)], out_recv.at[0])
    dq_ref[...] = interleave(query_tile)


def shards(query, key_in, value, output, grad_out, log_sum_exp):
    shape = query.shape
    flat = (shape[0] * shape[1], shape[2])
    arrays = [a.reshape(flat) for a in (query, key_in, value, output, grad_out)]
    dma = pltpu.SemaphoreType.DMA
    vmem = pl.BlockSpec(memory_space=pltpu.VMEM)
    grads = pl.pallas_call(
        kernel,
        out_shape=[jax.ShapeDtypeStruct(flat, BF)] * 3,
        in_specs=[vmem] * 6,
        out_specs=[vmem] * 3,
        scratch_shapes=[
            pltpu.VMEM((32, SLOT, 128), BF),
            pltpu.VMEM((32, SLOT, 128), BF),
            pltpu.VMEM((32, 1, 128), F32),
            pltpu.VMEM((8, ROWS, 128), BF),
            pltpu.VMEM((4, ROWS, 128), BF),
            pltpu.VMEM((32, 1, 128), F32),
            pltpu.VMEM((8, 2, ROWS), F32),
            pltpu.VMEM((4, ROWS, 128), BF),
            pltpu.VMEM((4, ROWS, 128), BF),
            pltpu.VMEM((4, 64, ROWS), BF),
            pltpu.VMEM((8, 64, ROWS), F32),
            pltpu.VMEM((4, ROWS, 128), F32),
            pltpu.VMEM((4, ROWS, 128), F32),
            pltpu.VMEM((6, 64, ROWS), BF),
            pltpu.VMEM((6, 64, ROWS), BF),
            pltpu.VMEM((2, ROWS, 128), BF),
            pltpu.VMEM((2, ROWS, 128), BF),
            pltpu.VMEM((32, 32, 128), BF),
            pltpu.VMEM((32, SLOT, 128), BF),
            pltpu.VMEM((32, 32, 128), BF),
            pltpu.VMEM((32, SLOT, 128), BF),
            dma((3,)), dma((6,)),
            dma((8,)), dma((8,)),
            dma((8,)), dma((8,)),
            dma((8,)), dma((8,)),
            dma((2,)), dma((2,)),
            dma((2,)), dma((2,)),
            dma((2,)), dma((2,)),
        ],
        compiler_params=pltpu.CompilerParams(
            collective_id=0, has_side_effects=True, vmem_limit_bytes=56 * 2**20
        ),
    )(*arrays, log_sum_exp)
    return tuple(g.reshape(shape) for g in grads)


def solution(mesh):
    rows = P(("blk", "head"), None, None)
    return jax.shard_map(
        shards,
        mesh=mesh,
        in_specs=(rows,) * 5 + (P(None, None, ("blk", "head")),),
        out_specs=(rows,) * 3,
        check_vma=False,
    )
```

time: 679 us -> 141 us (0.21)
  waiting for transfers between devices: 319 us -> 0 us
  matrix products: 179 us -> 0 us
  Pallas kernels: 0 us -> 130 us
  local copies, waits for them, and re-layouts: 97.8 us -> 8.99 us
  starting transfers between devices: 60.8 us -> 0 us
  other arithmetic: 17.5 us -> 0 us
    ppermute x64 -> x0, waiting for transfers between devices: 255 us -> none  [shifted(): return lax.ppermute(block, axis, route)]
    dot_general x80 -> x0, matrix products: 179 us -> none  [the longest x16 58.2 us: cycle_turn(): jnp.einsum('hsqk,kshd->qshd', grad_scores, keys_now, preferred_element_ty...]
    pallas_call x0 -> x1, Pallas kernels: none -> 130 us  [shards(): pl.pallas_call(kernel, out_shape=[jax.ShapeDtypeStruct(flat, BF)] * 3, in...]
    all_to_all x9 -> x0, waiting for transfers between devices: 63.2 us -> none  [the longest x1 10.1 us: shards(): lax.all_to_all(grad_q_low, 'head', split_axis=0, concat_axis=2, tiled=True)]
    all_to_all x9 -> x0, starting transfers between devices: 49.9 us -> none  [the longest x1 9.64 us: shards(): lax.all_to_all(grad_q_low, 'head', split_axis=0, concat_axis=2, tiled=True)]
    while x64 -> x0, local copies, waits for them, and re-layouts: 42 us -> none
    unnamed x28 -> x12, local copies, waits for them, and re-layouts: 20.5 us -> 0.6 us
    all_to_all x14 -> x0, local copies, waits for them, and re-layouts: 18.2 us -> none  [the longest x2 11.6 us: shards(): lax.all_to_all(grad_out, 'head', split_axis=2, concat_axis=0, tiled=True)]
  transfers between devices with their start and end apart: 73 -> 0, of which waited for: 39 -> 0; matrix products, arithmetic and copies ran while one was open for 22% -> 0% of each run, Pallas kernels for 0% -> 0%
where the time goes in v1:
time: 141 us; the launch traced here: 139 us
  Pallas kernels  130 us (92%)
  local copies, waits for them, and re-layouts  8.99 us (6%)
    pallas_call x1, Pallas kernels, shards(): pl.pallas_call(kernel, out_shape=[jax.ShapeDtypeStruct(flat, BF)] * 3, in...  130 us
    reshape x5, local copies, waits for them, and re-layouts, shards(): arrays = [a.reshape(flat) for a in (query, key_in, value, output, grad_out)]  4.99 us
    reshape x3, local copies, waits for them, and re-layouts, shards(): return tuple((g.reshape(shape) for g in grads))  3.4 us

profile of v1, /device:TPU:0, one launch (start us, length us, event | category | flops | bytes accessed | tf_op | source)
XLA Modules:
  0.0 139.2 jit_solution(11036761072888306699)
XLA Ops:
  0.6 0.0 copy-start
  0.6 1.8 %reshape.30.q_ref = bf16[128,1024]{1,0:T(8,128)(2,1)} reshape(bf16[64,2,1024]{2,1,0:T(2,128)(2,1)} %param.6) | data formatting | bytes 524288 | tf_op jit(solution)/shard_map/reshape | solution.py:345
  2.4 0.0 copy-done
  2.4 0.0 copy-start.1
  2.4 0.8 reshape.31.k_ref
  3.2 0.1 copy-done.1
  3.4 0.0 copy-start.2
  3.4 0.8 reshape.32.v_ref
  4.2 0.1 copy-done.2
  4.3 0.0 copy-start.3
  4.3 0.8 reshape.33.o_ref
  5.1 0.1 copy-done.3
  5.3 0.8 reshape.34.g_ref
  6.1 129.5 %shard_map.85 = (bf16[128,1024]{1,0:T(8,128)(2,1)}, bf16[128,1024]{1,0:T(8,128)(2,1)}, bf16[128,1024]{1,0:T(8,128)(2,1)}) custom-call(bf16[128,1024]{1,0:T(8,128)(2,1)} %reshape.30.q_ref, bf16[128,1024]{1,0:T(8,128)(2,1)} %reshape.31.k_ref, bf16[128,1024]{1,0:T(8,128)(2,1)} %reshape.32.v_ref, bf16[128,1024]{1,0:T(8,128)(2,1)} %reshape.33.o_ref, ...), custom_call_target="tpu_custom_call" | custom-call | tf_op jit(solution)/shard_map/pallas_call | solution.py:348
  135.6 0.0 copy-start.5
  135.6 1.8 %reshape.35 = bf16[64,2,1024]{2,1,0:T(2,128)(2,1)} reshape(bf16[128,1024]{1,0:T(8,128)(2,1)} %get-tuple-element.6) | data formatting | bytes 524288 | tf_op jit(solution)/shard_map/reshape | solution.py:387
  137.4 0.0 copy-done.5
  137.4 0.0 copy-start.4
  137.4 0.8 reshape.36
  138.2 0.1 copy-done.4
  138.4 0.8 reshape.37
Async XLA Ops:
  0.6 1.8 %copy-start = (bf16[64,2,1024]{2,1,0:T(2,128)(2,1)S(1)}, bf16[64,2,1024]{2,1,0:T(2,128)(2,1)}, u32[]{:S(2)}) copy-start(bf16[64,2,1024]{2,1,0:T(2,128)(2,1)} %param.7) | copy-start | bytes 786436
  2.4 1.0 copy-start.1
  3.4 0.9 copy-start.2
  4.3 0.9 copy-start.3
  135.6 1.8 %copy-start.5 = (bf16[128,1024]{1,0:T(8,128)(2,1)S(1)}, bf16[128,1024]{1,0:T(8,128)(2,1)}, u32[]{:S(2)}) copy-start(bf16[128,1024]{1,0:T(8,128)(2,1)} %get-tuple-element.7) | copy-start | bytes 786436
  137.4 1.0 copy-start.4

commit v2 on v1

--- a/solution.py
+++ b/solution.py
@@ -34,13 +34,13 @@
     return jnp.where(there == 2 * lax.rem(here, 64) + lax.div(here, 64), 1.0, 0.0).astype(BF)
 
 
-def place(high):
-    return jnp.where(iota((64, 128), 1) == iota((64, 128), 0) + (64 if high else 0), 1.0, 0.0).astype(BF)
+def eye(n):
+    return jnp.where(iota((n, n), 0) == iota((n, n), 1), 1.0, 0.0).astype(BF)
 
 
 def kernel(
     q_ref, k_ref, v_ref, o_ref, g_ref, lse_ref, dq_ref, dk_ref, dv_ref,
-    sq, sk, sa, qbuf, kbuf, ra, aux, kz, vz, kt, dqt, dka, dva,
+    sq, sk, sa, qbuf, kbuf, ra, aux, qz, gz, qgt, kzt, vzt, dqa, dkt, dvt,
     sdq, rdq, skv, rkv, oq, okv, iq, ikv,
     in_send, in_recv, ag_send, ag_recv, ax_send, ax_recv, dq_send, dq_recv,
     kx_send, kx_recv, dx_send, dx_recv, out_send, out_recv,
@@ -92,7 +92,7 @@
     to_seq = order_rows(False)
 
     def by_seq(ref):
-        return jnp.dot(to_seq, ref[...], preferred_element_type=F32)
+        return jnp.dot(to_seq, ref[...].reshape(128, 1024), preferred_element_type=F32)
 
     def pack(low, high, dst):
         for t in range(8):
@@ -115,8 +115,8 @@
     dots_rolled = roll_half(dots)
     for h in range(16):
         for s in range(2):
-            sa[2 * h + s, :, 0:64] = lse_ref[h, s:s + 1, :] * LOG2E
-            sa[2 * h + s, :, 64:128] = (dots if s else dots_rolled)[h:h + 1, 64:128]
+            sa[2 * h + s, :, 0:64] = lse_ref[h, s:s + 1, :] * (-1.0 / SCALE)
+            sa[2 * h + s, :, 64:128] = -(dots if s else dots_rolled)[h:h + 1, 64:128]
     pl.semaphore_wait(barrier, 35)
 
     def send_queries(n, c):
@@ -136,14 +136,13 @@
 
     lax.fori_loop(1, 16, send_queries, 0)
     pack(by_seq(k_ref), by_seq(v_ref), sk)
-    lax.fori_loop(1, 32, send_keys, 0)
-    lax.fori_loop(16, 32, send_queries, 0)
+    lax.fori_loop(1, 16, send_keys, 0)
     ra[0] = sa[my_pair]
     qbuf[0, 0:SLOT] = sq[my_pair]
     kbuf[0, 0:SLOT] = sk[my_pair]
-    dqt[...] = jnp.zeros_like(dqt)
-    dka[...] = jnp.zeros_like(dka)
-    dva[...] = jnp.zeros_like(dva)
+    dqa[...] = jnp.zeros_like(dqa)
+    dkt[...] = jnp.zeros_like(dkt)
+    dvt[...] = jnp.zeros_like(dvt)
 
     def queries_here(half):
         first = 0 if half else 1
@@ -164,13 +163,38 @@
         wait(aux.at[i], ax_recv.at[i])
 
     def prepare_keys(j):
-        both = kbuf[j]
+        turned = lax.dot_general(eye(128), kbuf[j], NT, preferred_element_type=F32)
+        row = iota((128, ROWS), 0)
+        ones = jnp.where(lax.rem(row, 64) < 3, 1.0, 0.0)
+        kzt[j] = jnp.where(row < 64, turned, ones).astype(BF)
+        vzt[j] = jnp.where(row < 64, ones, turned).astype(BF)
+
+    def prepare_queries(i):
+        rest, parts = aux[i], []
+        for _ in range(3):
+            parts.append(rest.astype(BF).astype(F32))
+            rest = rest - parts[-1]
+        parts = jnp.concatenate(parts + [jnp.zeros((10, ROWS), F32)], 0).astype(BF)
+        row, lane = iota((16, 128), 0), iota((16, 128), 1)
+        spot = 64 * (1 - lax.rem(row, 2)) + lax.div(row, 2)
+        spare = jnp.where((lane == spot) & (row < 6), 1.0, 0.0).astype(BF)
+        columns = lax.dot_general(parts, spare, TN, preferred_element_type=F32).astype(BF)
+        both = qbuf[i]
         low = low_half(ROWS)
-        zero = jnp.zeros_like(both)
-        kz[j] = jnp.where(low, both, zero)
-        vz[j] = jnp.where(low, zero, both)
-        eye = jnp.where(iota((64, 128), 0) == iota((64, 128), 1), 1.0, 0.0).astype(BF)
-        kt[j] = lax.dot_general(eye, both, NT, preferred_element_type=F32).astype(BF)
+        qz[...] = jnp.where(low, both, columns)
+        gz[...] = jnp.where(low, columns, both)
+        qgt[...] = lax.dot_general(eye(128), both, NT, preferred_element_type=F32).astype(BF)
+
+    def front(j):
+        scores = jnp.dot(qz[...], kzt[j], preferred_element_type=F32)
+        grad_probs = jnp.dot(gz[...], vzt[j], preferred_element_type=F32)
+        probs = jnp.exp2(scores * (SCALE * LOG2E))
+        return probs.astype(BF), (probs * grad_probs).astype(BF)
+
+    def back(i, j, probs, grad_scores):
+        dvt[j] += jnp.dot(qgt[64:128], probs, preferred_element_type=F32)
+        dkt[j] += jnp.dot(qgt[0:64], grad_scores, preferred_element_type=F32)
+        dqa[i] += jnp.dot(grad_scores, kbuf[j], preferred_element_type=F32)
 
     def keys_here(j):
         if j < 2:
@@ -182,7 +206,10 @@
         prepare_keys(j)
 
     def both_grads(j):
-        return jnp.where(low_half(ROWS), dka[j] * SCALE, dva[j])
+        return jnp.concatenate([dkt[j] * SCALE, dvt[j]], 0)
+
+    def packed_queries(i):
+        return jnp.where(low_half(ROWS // 2), dqa[i, 0:ROWS // 2], roll_half(dqa[i, ROWS // 2:ROWS]))
 
     def send_out(lo, hi, src, dst, which):
         def one(n, c):
@@ -196,22 +223,22 @@
             dst[my_pair] = src[0]
 
     def finish_queries(half):
-        parts = (3, 4, 6) if half else (1, 2, 5)
-        total = dqt[7 * half]
-        for i in parts:
+        total = packed_queries(7 * half)
+        for i in (3, 5, 6) if half else (1, 2, 4):
             wait(rdq.at[i - 1], dq_recv.at[i])
             total = total + rdq[i - 1].astype(F32)
-        low = (total * SCALE).astype(BF)
-        a = lax.dot_general(low, place(False), TN, preferred_element_type=F32)
-        b = lax.dot_general(low, place(True), TN, preferred_element_type=F32)
-        for n in range(16):
-            both = a[n * 64:n * 64 + 32] + b[n * 64 + 32:n * 64 + 64]
-            oq[16 * half + n] = both.astype(BF)
+        total = total * SCALE
+        low = low_half(32)
+        for n in range(8):
+            a, b = total[n * 64:n * 64 + 32], total[n * 64 + 32:n * 64 + 64]
+            oq[16 * half + n] = jnp.where(low, a, roll_half(b)).astype(BF)
+            oq[16 * half + 8 + n] = jnp.where(low, roll_half(a), b).astype(BF)
         send_out(16 * half, 16 * half + 16, oq, iq, 0)
 
     def finish_keys(j):
         wait(rkv.at[j], dx_recv.at[j])
         total = (both_grads(j) + rkv[j].astype(F32)).astype(BF)
+        total = lax.dot_general(total, eye(128), TN, preferred_element_type=F32).astype(BF)
         for n in range(16):
             okv[16 * j + n] = total[n * 64:(n + 1) * 64]
         send_out(16 * j, 16 * j + 16, okv, ikv, 1)
@@ -220,84 +247,90 @@
     pass_chunk(0, 1, 3)
     pass_chunk(0, 2, 1)
     keys_here(0)
-
-    def turn(t, c):
-        i = lax.div(t, 4)
-        j = lax.rem(lax.rem(t, 4) + 2 * lax.div(i, 7), 4)
+    lax.fori_loop(16, 32, send_keys, 0)
+
+    def start_turn(t, c):
+        i, r = 7 * lax.div(t, 4), lax.rem(t, 4)
+        second = lax.div(t, 4)
+        j = (1 - second) * (lax.div(r, 2) + 2 * lax.rem(r, 2)) + second * (r + 2)
+
+        @pl.when(t == 0)
+        def _():
+            prepare_queries(0)
 
         @pl.when(t == 1)
         def _():
+            lax.fori_loop(16, 32, send_queries, 0)
+            keys_here(2)
+
+        @pl.when(t == 2)
+        def _():
             keys_here(1)
+
+        @pl.when(t == 3)
+        def _():
+            keys_here(3)
+
+        @pl.when(t == 4)
+        def _():
             queries_here(1)
             pass_chunk(7, 3, 3)
-            pass_chunk(7, 4, 1)
-
-        @pl.when(t == 2)
-        def _():
-            keys_here(2)
-
-        @pl.when(t == 3)
-        def _():
-            keys_here(3)
-
-        @pl.when(t == 4)
+            pass_chunk(7, 6, 1)
+            prepare_queries(7)
+
+        back(i, j, *front(j))
+        return c
+
+    lax.fori_loop(0, 6, start_turn, 0)
+
+    def middle_turn(i, c):
+        @pl.when(i == 1)
         def _():
             chunk_here(1)
-            pass_chunk(1, 5, 3)
-
-        @pl.when(t == 8)
+            pass_chunk(1, 4, 3)
+
+        @pl.when(i == 2)
         def _():
             chunk_here(2)
 
-        @pl.when(t == 12)
+        @pl.when(i == 3)
         def _():
             chunk_here(3)
-            chunk_here(4)
-            pass_chunk(4, 6, 1)
-
-        @pl.when(t == 20)
-        def _():
-            chunk_here(5)
-
-        @pl.when(t == 24)
-        def _():
             chunk_here(6)
-
-        @pl.when(t == 30)
-        def _():
-            finish_queries(0)
-
-        rows = qbuf[i]
-        scores = lax.dot_general(kz[j], rows, NT, preferred_element_type=F32)
-        grad_probs = lax.dot_general(vz[j], rows, NT, preferred_element_type=F32)
-        probs = jnp.exp2(scores * (SCALE * LOG2E) - aux[i, 0:1, :])
-        grad_scores = (probs * (grad_probs - aux[i, 1:2, :])).astype(BF)
-        dva[j] += jnp.dot(probs.astype(BF), rows, preferred_element_type=F32)
-        dka[j] += jnp.dot(grad_scores, rows, preferred_element_type=F32)
-        dqt[i] += jnp.dot(kt[j], grad_scores, preferred_element_type=F32)
-
-        for i_done, distance in ((1, 1), (2, 3), (3, 1), (4, 3), (5, 2), (6, 2)):
-
-            @pl.when(t == 4 * i_done + 3)
+            pass_chunk(6, 5, 1)
+
+        for late in (4, 5):
+
+            @pl.when(i == late)
             def _():
-                sdq[i_done - 1] = dqt[i_done].astype(BF)
-                send(sdq.at[i_done - 1], rdq.at[i_done - 1], dq_send.at[i_done], dq_recv.at[i_done], ring(distance)).start()
-
-        for half in range(2):
-
-            @pl.when(t == 28 + half)
+                chunk_here(late)
+
+        prepare_queries(i)
+        now = front(0)
+        for j in range(4):
+            later = front(j + 1) if j < 3 else None
+            back(i, j, *now)
+            now = later
+        sdq[i - 1] = packed_queries(i).astype(BF)
+
+        for done, distance in ((1, 1), (2, 3), (3, 1), (4, 2), (5, 2), (6, 3)):
+
+            @pl.when(i == done)
             def _():
-                skv[half] = both_grads(2 + half).astype(BF)
-                send(skv.at[half], rkv.at[half], dx_send.at[half], dx_recv.at[half], partner).start()
-
-        @pl.when(t == 30)
-        def _():
-            finish_keys(0)
+                send(sdq.at[done - 1], rdq.at[done - 1], dq_send.at[done], dq_recv.at[done], ring(distance)).start()
 
         return c
 
-    lax.fori_loop(0, 32, turn, 0)
-    finish_keys(1)
+    lax.fori_loop(1, 7, middle_turn, 0)
+    for half in range(2):
+        skv[half] = both_grads(2 + half).astype(BF)
+        send(skv.at[half], rkv.at[half], dx_send.at[half], dx_recv.at[half], partner).start()
+    prepare_queries(7)
+    finish_queries(0)
+
+    for j in range(2):
+        back(7, j, *front(j))
+        finish_keys(j)
     finish_queries(1)
 
     wait(sa.at[pl.ds(0, 31)], in_send.at[0])
@@ -317,7 +350,8 @@
 
     def interleave(tiles):
         rows = jnp.concatenate([jnp.concatenate([tiles(s, t) for t in range(8)], 1) for s in range(2)], 0)
-        return jnp.dot(to_frames, rows.astype(BF), preferred_element_type=F32).astype(BF)
+        rows = jnp.dot(to_frames, rows.astype(BF), preferred_element_type=F32).astype(BF)
+        return rows.reshape(64, 2, 1024)
 
     wait(ikv.at[pl.ds(0, 31)], out_recv.at[1])
 
@@ -340,14 +374,11 @@
 
 
 def shards(query, key_in, value, output, grad_out, log_sum_exp):
-    shape = query.shape
-    flat = (shape[0] * shape[1], shape[2])
-    arrays = [a.reshape(flat) for a in (query, key_in, value, output, grad_out)]
     dma = pltpu.SemaphoreType.DMA
     vmem = pl.BlockSpec(memory_space=pltpu.VMEM)
-    grads = pl.pallas_call(
+    return pl.pallas_call(
         kernel,
-        out_shape=[jax.ShapeDtypeStruct(flat, BF)] * 3,
+        out_shape=[jax.ShapeDtypeStruct(query.shape, BF)] * 3,
         in_specs=[vmem] * 6,
         out_specs=[vmem] * 3,
         scratch_shapes=[
@@ -358,16 +389,18 @@
             pltpu.VMEM((4, ROWS, 128), BF),
             pltpu.VMEM((32, 1, 128), F32),
             pltpu.VMEM((8, 2, ROWS), F32),
-            pltpu.VMEM((4, ROWS, 128), BF),
-            pltpu.VMEM((4, ROWS, 128), BF),
-            pltpu.VMEM((4, 64, ROWS), BF),
-            pltpu.VMEM((8, 64, ROWS), F32),
-            pltpu.VMEM((4, ROWS, 128), F32),
-            pltpu.VMEM((4, ROWS, 128), F32),
-            pltpu.VMEM((6, 64, ROWS), BF),
-            pltpu.VMEM((6, 64, ROWS), BF),
-            pltpu.VMEM((2, ROWS, 128), BF),
-            pltpu.VMEM((2, ROWS, 128), BF),
+            pltpu.VMEM((ROWS, 128), BF),
+            pltpu.VMEM((ROWS, 128), BF),
+            pltpu.VMEM((128, ROWS), BF),
+            pltpu.VMEM((4, 128, ROWS), BF),
+            pltpu.VMEM((4, 128, ROWS), BF),
+            pltpu.VMEM((8, ROWS, 128), F32),
+            pltpu.VMEM((4, 64, ROWS), F32),
+            pltpu.VMEM((4, 64, ROWS), F32),
+            pltpu.VMEM((6, ROWS // 2, 128), BF),
+            pltpu.VMEM((6, ROWS // 2, 128), BF),
+            pltpu.VMEM((2, 128, ROWS), BF),
+            pltpu.VMEM((2, 128, ROWS), BF),
             pltpu.VMEM((32, 32, 128), BF),
             pltpu.VMEM((32, SLOT, 128), BF),
             pltpu.VMEM((32, 32, 128), BF),
@@ -383,8 +416,7 @@
         compiler_params=pltpu.CompilerParams(
             collective_id=0, has_side_effects=True, vmem_limit_bytes=56 * 2**20
         ),
-    )(*arrays, log_sum_exp)
-    return tuple(g.reshape(shape) for g in grads)
+    )(query, key_in, value, output, grad_out, log_sum_exp)
 
 
 def solution(mesh):

time: 141 us -> 130 us (0.922)
  Pallas kernels: 130 us -> 124 us
  local copies, waits for them, and re-layouts: 8.99 us -> 3.63 us
    reshape x8 -> x0, local copies, waits for them, and re-layouts: 8.39 us -> none  [the longest x5 4.99 us: shards(): arrays = [a.reshape(flat) for a in (query, key_in, value, output, grad_out)]]
    pallas_call x1, Pallas kernels: 130 us -> 124 us  [shards(): pl.pallas_call(kernel, out_shape=[jax.ShapeDtypeStruct(query.shape, BF)]...]
    unnamed x12 -> x7, local copies, waits for them, and re-layouts: 0.6 us -> 3.63 us
where the time goes in v2:
time: 130 us; the launch traced here: 128 us
  Pallas kernels  124 us (95%)
  local copies, waits for them, and re-layouts  3.63 us (3%)
    pallas_call x1, Pallas kernels, shards(): pl.pallas_call(kernel, out_shape=[jax.ShapeDtypeStruct(query.shape, BF)]...  124 us
    unnamed x7, local copies, waits for them, and re-layouts  3.63 us

profile of v2, /device:TPU:0, one launch (start us, length us, event | category | flops | bytes accessed | tf_op | source)
XLA Modules:
  0.0 128.2 jit_solution(4600680601114668639)
XLA Ops:
  0.6 124.0 %shard_map.85 = (bf16[64,2,1024]{2,1,0:T(2,128)(2,1)}, bf16[64,2,1024]{2,1,0:T(2,128)(2,1)}, bf16[64,2,1024]{2,1,0:T(2,128)(2,1)}) custom-call(bf16[64,2,1024]{2,1,0:T(2,128)(2,1)} %q_ref.1, bf16[64,2,1024]{2,1,0:T(2,128)(2,1)} %k_ref.1, bf16[64,2,1024]{2,1,0:T(2,128)(2,1)} %v_ref.1, bf16[64,2,1024]{2,1,0:T(2,128)(2,1)} %o_ref.1, ...), custom_call_target="tpu_custom_call" | custom-call | tf_op jit(solution)/shard_map/pallas_call | solution.py:379
  124.6 0.0 copy-start.1
  124.6 1.9 %copy.12 = bf16[64,2,1024]{2,1,0:T(2,128)(2,1)} copy(bf16[64,2,1024]{2,1,0:T(2,128)(2,1)} %get-tuple-element.6) | data formatting | bytes 524288
  126.5 0.0 copy-done.1
  126.5 0.0 copy-start
  126.5 0.7 copy.13
  127.2 0.3 copy-done
  127.5 0.7 copy.14
Async XLA Ops:
  124.6 1.9 %copy-start.1 = (bf16[64,2,1024]{2,1,0:T(2,128)(2,1)S(1)}, bf16[64,2,1024]{2,1,0:T(2,128)(2,1)}, u32[]{:S(2)}) copy-start(bf16[64,2,1024]{2,1,0:T(2,128)(2,1)} %get-tuple-element.7) | copy-start | bytes 786436
  126.5 1.0 copy-start

commit v3 on v2

--- a/solution.py
+++ b/solution.py
@@ -39,9 +39,9 @@
 
 
 def kernel(
-    q_ref, k_ref, v_ref, o_ref, g_ref, lse_ref, dq_ref, dk_ref, dv_ref,
+    q_ref, k_ref, v_ref, o_ref, g_ref, lse_ref, iq, ikv,
     sq, sk, sa, qbuf, kbuf, ra, aux, qz, gz, qgt, kzt, vzt, dqa, dkt, dvt,
-    sdq, rdq, skv, rkv, oq, okv, iq, ikv,
+    sdq, rdq, skv, rkv, oq, okv,
     in_send, in_recv, ag_send, ag_recv, ax_send, ax_recv, dq_send, dq_recv,
     kx_send, kx_recv, dx_send, dx_recv, out_send, out_recv,
 ):
@@ -185,16 +185,16 @@
         gz[...] = jnp.where(low, columns, both)
         qgt[...] = lax.dot_general(eye(128), both, NT, preferred_element_type=F32).astype(BF)
 
-    def front(j):
-        scores = jnp.dot(qz[...], kzt[j], preferred_element_type=F32)
-        grad_probs = jnp.dot(gz[...], vzt[j], preferred_element_type=F32)
+    def front(j, part=slice(0, ROWS)):
+        scores = jnp.dot(qz[...], kzt[j, :, part], preferred_element_type=F32)
+        grad_probs = jnp.dot(gz[...], vzt[j, :, part], preferred_element_type=F32)
         probs = jnp.exp2(scores * (SCALE * LOG2E))
         return probs.astype(BF), (probs * grad_probs).astype(BF)
 
-    def back(i, j, probs, grad_scores):
-        dvt[j] += jnp.dot(qgt[64:128], probs, preferred_element_type=F32)
-        dkt[j] += jnp.dot(qgt[0:64], grad_scores, preferred_element_type=F32)
-        dqa[i] += jnp.dot(grad_scores, kbuf[j], preferred_element_type=F32)
+    def back(i, j, probs, grad_scores, part=slice(0, ROWS)):
+        dvt[j, :, part] += jnp.dot(qgt[64:128], probs, preferred_element_type=F32)
+        dkt[j, :, part] += jnp.dot(qgt[0:64], grad_scores, preferred_element_type=F32)
+        dqa[i] += jnp.dot(grad_scores, kbuf[j, part], preferred_element_type=F32)
 
     def keys_here(j):
         if j < 2:
@@ -235,13 +235,14 @@
             oq[16 * half + 8 + n] = jnp.where(low, roll_half(a), b).astype(BF)
         send_out(16 * half, 16 * half + 16, oq, iq, 0)
 
-    def finish_keys(j):
-        wait(rkv.at[j], dx_recv.at[j])
-        total = (both_grads(j) + rkv[j].astype(F32)).astype(BF)
-        total = lax.dot_general(total, eye(128), TN, preferred_element_type=F32).astype(BF)
-        for n in range(16):
-            okv[16 * j + n] = total[n * 64:(n + 1) * 64]
-        send_out(16 * j, 16 * j + 16, okv, ikv, 1)
+    def finish_keys(j, part):
+        total = jnp.concatenate([dkt[j, :, part] * SCALE, dvt[j, :, part]], 0) + rkv[j, :, part].astype(F32)
+        total = lax.dot_general(total.astype(BF), eye(128), TN, preferred_element_type=F32).astype(BF)
+        first = (ROWS * j + part.start) // SLOT
+        count = (part.stop - part.start) // SLOT
+        for n in range(count):
+            okv[first + n] = total[n * SLOT:(n + 1) * SLOT]
+        send_out(first, first + count, okv, ikv, 1)
 
     queries_here(0)
     pass_chunk(0, 1, 3)
@@ -329,8 +330,11 @@
     finish_queries(0)
 
     for j in range(2):
-        back(7, j, *front(j))
-        finish_keys(j)
+        for part in (slice(0, ROWS // 2), slice(ROWS // 2, ROWS)):
+            back(7, j, *front(j, part), part)
+            if part.start == 0:
+                wait(rkv.at[j], dx_recv.at[j])
+            finish_keys(j, part)
     finish_queries(1)
 
     wait(sa.at[pl.ds(0, 31)], in_send.at[0])
@@ -346,14 +350,17 @@
     wait(oq.at[pl.ds(0, 31)], out_send.at[0])
     wait(okv.at[pl.ds(0, 31)], out_send.at[1])
 
+    wait(ikv.at[pl.ds(0, 31)], out_recv.at[1])
+    wait(iq.at[pl.ds(0, 31)], out_recv.at[0])
+
+
+def unpack(iq, ikv, dq_ref, dk_ref, dv_ref):
     to_frames = order_rows(True)
 
     def interleave(tiles):
         rows = jnp.concatenate([jnp.concatenate([tiles(s, t) for t in range(8)], 1) for s in range(2)], 0)
         rows = jnp.dot(to_frames, rows.astype(BF), preferred_element_type=F32).astype(BF)
         return rows.reshape(64, 2, 1024)
-
-    wait(ikv.at[pl.ds(0, 31)], out_recv.at[1])
 
     def key_tile(s, t):
         return jnp.where(low_half(64), ikv[4 * t + s].astype(F32), roll_half(ikv[4 * t + 2 + s].astype(F32)))
@@ -369,18 +376,18 @@
 
     dk_ref[...] = interleave(key_tile)
     dv_ref[...] = interleave(value_tile)
-    wait(iq.at[pl.ds(0, 31)], out_recv.at[0])
     dq_ref[...] = interleave(query_tile)
 
 
 def shards(query, key_in, value, output, grad_out, log_sum_exp):
     dma = pltpu.SemaphoreType.DMA
     vmem = pl.BlockSpec(memory_space=pltpu.VMEM)
-    return pl.pallas_call(
+    back_here = [jax.ShapeDtypeStruct((32, 32, 128), BF), jax.ShapeDtypeStruct((32, SLOT, 128), BF)]
+    parts = pl.pallas_call(
         kernel,
-        out_shape=[jax.ShapeDtypeStruct(query.shape, BF)] * 3,
+        out_shape=back_here,
         in_specs=[vmem] * 6,
-        out_specs=[vmem] * 3,
+        out_specs=[vmem] * 2,
         scratch_shapes=[
             pltpu.VMEM((32, SLOT, 128), BF),
             pltpu.VMEM((32, SLOT, 128), BF),
@@ -403,8 +410,6 @@
             pltpu.VMEM((2, 128, ROWS), BF),
             pltpu.VMEM((32, 32, 128), BF),
             pltpu.VMEM((32, SLOT, 128), BF),
-            pltpu.VMEM((32, 32, 128), BF),
-            pltpu.VMEM((32, SLOT, 128), BF),
             dma((3,)), dma((6,)),
             dma((8,)), dma((8,)),
             dma((8,)), dma((8,)),
@@ -417,6 +422,12 @@
             collective_id=0, has_side_effects=True, vmem_limit_bytes=56 * 2**20
         ),
     )(query, key_in, value, output, grad_out, log_sum_exp)
+    return pl.pallas_call(
+        unpack,
+        out_shape=[jax.ShapeDtypeStruct(query.shape, BF)] * 3,
+        in_specs=[vmem] * 2,
+        out_specs=[vmem] * 3,
+    )(*parts)
 
 
 def solution(mesh):

time: 130 us -> 128 us (0.985)
  local copies, waits for them, and re-layouts: 3.63 us -> 0 us
  Pallas kernels: 124 us -> 126 us
    unnamed x7 -> x0, local copies, waits for them, and re-layouts: 3.63 us -> none
    pallas_call x1 -> x2, Pallas kernels: 124 us -> 126 us  [the longest x1 124 us: shards(): pl.pallas_call(kernel, out_shape=back_here, in_specs=[vmem] * 6, out_spec...]
where the time goes in v3:
time: 128 us; the launch traced here: 127 us
  Pallas kernels  126 us (98%)
    pallas_call x1, Pallas kernels, shards(): pl.pallas_call(kernel, out_shape=back_here, in_specs=[vmem] * 6, out_spec...  124 us

profile of v3, /device:TPU:0, one launch (start us, length us, event | category | flops | bytes accessed | tf_op | source)
XLA Modules:
  0.0 126.8 jit_solution(7133802180989477408)
XLA Ops:
  0.6 123.7 %shard_map.85 = (bf16[32,32,128]{2,1,0:T(8,128)(2,1)}, bf16[32,64,128]{2,1,0:T(8,128)(2,1)}) custom-call(bf16[64,2,1024]{2,1,0:T(2,128)(2,1)} %q_ref.1, bf16[64,2,1024]{2,1,0:T(2,128)(2,1)} %k_ref.1, bf16[64,2,1024]{2,1,0:T(2,128)(2,1)} %v_ref.1, bf16[64,2,1024]{2,1,0:T(2,128)(2,1)} %o_ref.1, bf16[64,2,1024]{2,1,0:T(2,128)(2,1)} %g_ref.1, f32[16,2,64]{2,1,0:T(2,128)} %lse_ref.1), custom_call_target="tpu_custom_call" | custom-call | tf_op jit(solution)/shard_map/pallas_call | solution.py:386
  124.4 2.4 %shard_map.86 = (bf16[64,2,1024]{2,1,0:T(2,128)(2,1)}, bf16[64,2,1024]{2,1,0:T(2,128)(2,1)}, bf16[64,2,1024]{2,1,0:T(2,128)(2,1)}) custom-call(bf16[32,32,128]{2,1,0:T(8,128)(2,1)} %get-tuple-element.5.iq, bf16[32,64,128]{2,1,0:T(8,128)(2,1)} %get-tuple-element.6.ikv), custom_call_target="tpu_custom_call" | custom-call | tf_op jit(solution)/shard_map/pallas_call | solution.py:425

commit v4 on v3

--- a/solution.py
+++ b/solution.py
@@ -251,9 +251,7 @@
     lax.fori_loop(16, 32, send_keys, 0)
 
     def start_turn(t, c):
-        i, r = 7 * lax.div(t, 4), lax.rem(t, 4)
-        second = lax.div(t, 4)
-        j = (1 - second) * (lax.div(r, 2) + 2 * lax.rem(r, 2)) + second * (r + 2)
+        j = lax.div(t, 2) + 2 * lax.rem(t, 2)
 
         @pl.when(t == 0)
         def _():
@@ -272,17 +270,18 @@
         def _():
             keys_here(3)
 
-        @pl.when(t == 4)
-        def _():
-            queries_here(1)
-            pass_chunk(7, 3, 3)
-            pass_chunk(7, 6, 1)
-            prepare_queries(7)
-
-        back(i, j, *front(j))
+        back(0, j, *front(j))
         return c
 
-    lax.fori_loop(0, 6, start_turn, 0)
+    lax.fori_loop(0, 4, start_turn, 0)
+
+    queries_here(1)
+    pass_chunk(7, 3, 3)
+    pass_chunk(7, 6, 1)
+    prepare_queries(7)
+    now, later = front(2), front(3)
+    back(7, 2, *now)
+    back(7, 3, *later)
 
     def middle_turn(i, c):
         @pl.when(i == 1)

time: 128 us -> 128 us (level)
  no operation moved by 1% of the time
where the time goes in v4:
time: 128 us; the launch traced here: 127 us
  Pallas kernels  126 us (98%)
    pallas_call x1, Pallas kernels, shards(): pl.pallas_call(kernel, out_shape=back_here, in_specs=[vmem] * 6, out_spec...  124 us

profile of v4, /device:TPU:0, one launch (start us, length us, event | category | flops | bytes accessed | tf_op | source)
XLA Modules:
  0.0 126.7 jit_solution(12326876380081504746)
XLA Ops:
  0.6 123.7 %shard_map.85 = (bf16[32,32,128]{2,1,0:T(8,128)(2,1)}, bf16[32,64,128]{2,1,0:T(8,128)(2,1)}) custom-call(bf16[64,2,1024]{2,1,0:T(2,128)(2,1)} %q_ref.1, bf16[64,2,1024]{2,1,0:T(2,128)(2,1)} %k_ref.1, bf16[64,2,1024]{2,1,0:T(2,128)(2,1)} %v_ref.1, bf16[64,2,1024]{2,1,0:T(2,128)(2,1)} %o_ref.1, bf16[64,2,1024]{2,1,0:T(2,128)(2,1)} %g_ref.1, f32[16,2,64]{2,1,0:T(2,128)} %lse_ref.1), custom_call_target="tpu_custom_call" | custom-call | tf_op jit(solution)/shard_map/pallas_call | solution.py:385
  124.4 2.4 %shard_map.86 = (bf16[64,2,1024]{2,1,0:T(2,128)(2,1)}, bf16[64,2,1024]{2,1,0:T(2,128)(2,1)}, bf16[64,2,1024]{2,1,0:T(2,128)(2,1)}) custom-call(bf16[32,32,128]{2,1,0:T(8,128)(2,1)} %get-tuple-element.5.iq, bf16[32,64,128]{2,1,0:T(8,128)(2,1)} %get-tuple-element.6.ikv), custom_call_target="tpu_custom_call" | custom-call | tf_op jit(solution)/shard_map/pallas_call | solution.py:424
